TPU v7x, 32 devices: a whole 2x2x4 slice. The times are simulated.
32 devices in a mesh: rep: 4 (over y, x), ep: 8 (over z, core).
Axes of the slice: x: 2, y: 2, z: 4, core: 2. Of those that a mesh axis runs over, the one named last changes fastest.
Arguments:
- q_latent: bfloat16 [256, 128, 512], P(('rep', 'ep')), may hold values from -6 to 6
- q_rope: bfloat16 [256, 128, 64], P(('rep', 'ep')), may hold values from -104 to 104
- cache_latent: bfloat16 [256, 128, 512], P(('rep', 'ep')), may hold values from -6 to 6
- cache_rope: bfloat16 [256, 128, 64], P(('rep', 'ep')), may hold values from -6 to 6
- cache_len: int32 [256], P(('rep', 'ep')), may hold values from 32 to 128, as said below
- stream: bfloat16 [256, 7168], P(('rep', 'ep')), may hold values from -6 to 6
- norm_gain: float32 [7168], replicated, may hold values from 0.1 to 1.9
- expert_ids: int32 [256, 8], P(('rep', 'ep')), may hold values from 0 to 15, all different within a row; in each aligned block of 8 rows (0 to 7, 8 to 15, ...) at most 8 rows name the same one
- route_weights: bfloat16 [256, 8], P(('rep', 'ep')), may hold values from 0.099609375 to 1
- w_gate: bfloat16 [16, 7168, 1024], P('ep', None, 'rep'), may hold values from -0.0625 to 0.0625
- w_up: bfloat16 [16, 7168, 1024], P('ep', None, 'rep'), may hold values from -0.0625 to 0.0625
- w_down: bfloat16 [16, 1024, 7168], P('ep', 'rep'), may hold values from -0.1875 to 0.1875
Outputs:
- attn_latent: bfloat16 [256, 128, 512], P(('rep', 'ep'))
- layer_out: bfloat16 [256, 7168], P(('rep', 'ep'))
Inputs may be any that keep to these rules, and one draw needn't show every extreme that they name: `expert_ids`: each row names 8 different experts; within the rows of one device no expert is named by more than 8 rows, a bound that some block reaches. `cache_len`: some row has all 128 positions live.
All inputs are finite; a program needn't handle non-finite values.
Results may differ from a plain program's by a relative error of at most 0.01.
Values may be sent and summed in bfloat16 or wider, within the bound.
A program may use at most 128 MiB of HBM per device.

v0:
```python
import jax
import jax.numpy as jnp
from jax import lax
from jax.sharding import PartitionSpec as P

score_scale = 192.0 ** (-0.5)
norm_eps = 1e-06


def slot_ranks(route_table, expert_total):
    onehot = (route_table[..., None] == jnp.arange(expert_total, dtype=jnp.int32)).astype(jnp.int32)
    earlier = jnp.cumsum(onehot, axis=1) - onehot
    return jnp.sum(earlier * onehot, axis=-1)


def fill_slots(features, slot_index, row_index, slot_total):
    sources = jnp.zeros((slot_total,), jnp.int32).at[slot_index].set(row_index)
    filled = jnp.zeros((slot_total,), features.dtype).at[slot_index].set(1)
    return features[sources] * filled[:, None]


def expert_block(tokens_in, gate_part, up_part, down_part):
    gate_act = jnp.dot(tokens_in, gate_part, preferred_element_type=jnp.float32)
    up_act = jnp.dot(tokens_in, up_part, preferred_element_type=jnp.float32)
    hidden = (jax.nn.silu(gate_act) * up_act).astype(jnp.bfloat16)
    return jnp.dot(hidden, down_part, preferred_element_type=jnp.float32).astype(jnp.bfloat16)


def per_device(
    q_latent,
    q_rope,
    cache_latent,
    cache_rope,
    cache_len,
    stream,
    norm_gain,
    expert_ids,
    route_weights,
    w_gate,
    w_up,
    w_down,
):
    ep_count = lax.axis_size("ep")
    row_count, feature_dim = stream.shape
    local_count = w_gate.shape[0]
    top_count = expert_ids.shape[1]
    expert_total = local_count * ep_count
    capacity = max(2, 2 * row_count * top_count // expert_total)
    stream_f = stream.astype(jnp.float32)
    normed = (
        stream_f
        * lax.rsqrt(jnp.mean(stream_f * stream_f, axis=-1, keepdims=True) + norm_eps)
        * norm_gain
    ).astype(jnp.bfloat16)
    flat_routes = expert_ids.reshape(-1)
    rank_in = slot_ranks(flat_routes.reshape(1, -1), expert_total)[0]
    expert_slot = flat_routes % local_count * ep_count + flat_routes // local_count
    slot_index = expert_slot * capacity + rank_in
    row_index = jnp.arange(row_count * top_count, dtype=jnp.int32) // top_count
    slot_total = expert_total * capacity
    outgoing = fill_slots(normed, slot_index, row_index, slot_total).reshape(
        local_count, ep_count, capacity, feature_dim
    )
    incoming = lax.all_to_all(outgoing, "ep", split_axis=1, concat_axis=1, tiled=True)
    incoming = incoming.reshape(local_count, ep_count * capacity, feature_dim)
    scores = (
        jnp.einsum("ihl,itl->iht", q_latent, cache_latent, preferred_element_type=jnp.float32)
        + jnp.einsum("ihr,itr->iht", q_rope, cache_rope, preferred_element_type=jnp.float32)
    ) * score_scale
    valid_mask = (
        jnp.arange(cache_latent.shape[1], dtype=jnp.int32)[None, None, :] < cache_len[:, None, None]
    )
    scores = jnp.where(valid_mask, scores, -1e30)
    top_score = jnp.max(scores, axis=-1, keepdims=True)
    exponent = jnp.where(valid_mask, jnp.exp(scores - top_score), 0.0)
    attn_weights = (exponent / jnp.sum(exponent, axis=-1, keepdims=True)).astype(jnp.bfloat16)
    attn_latent = jnp.einsum(
        "iht,itl->ihl", attn_weights, cache_latent, preferred_element_type=jnp.float32
    ).astype(jnp.bfloat16)
    everyone = lax.all_gather(incoming, "rep", axis=1, tiled=True)
    partials = jax.vmap(expert_block)(everyone, w_gate, w_up, w_down)
    partials = lax.optimization_barrier(partials)
    summed = lax.psum_scatter(
        partials.astype(jnp.float32).astype(jnp.bfloat16), "rep", scatter_dimension=1, tiled=True
    ).astype(jnp.float32)
    returned = lax.all_to_all(
        summed.reshape(local_count, ep_count, capacity, feature_dim).astype(jnp.bfloat16),
        "ep",
        split_axis=1,
        concat_axis=1,
        tiled=True,
    ).astype(jnp.float32)
    picked = returned.reshape(slot_total, feature_dim)[slot_index].reshape(
        row_count, top_count, feature_dim
    )
    expert_sum = jnp.einsum(
        "rk,rkd->rd", route_weights.astype(jnp.float32), picked, precision=lax.Precision.HIGHEST
    )
    layer_out = (stream_f + expert_sum).astype(jnp.bfloat16)
    return (attn_latent, layer_out)


def solution(mesh):
    placed = (
        P(("rep", "ep"), None, None),
        P(("rep", "ep"), None, None),
        P(("rep", "ep"), None, None),
        P(("rep", "ep"), None, None),
        P(("rep", "ep")),
        P(("rep", "ep"), None),
        P(),
        P(("rep", "ep"), None),
        P(("rep", "ep"), None),
        P("ep", None, "rep"),
        P("ep", None, "rep"),
        P("ep", "rep", None),
    )
    return jax.shard_map(
        per_device,
        mesh=mesh,
        in_specs=placed,
        out_specs=(P(("rep", "ep"), None, None), P(("rep", "ep"), None)),
        check_vma=False,
    )
```

profile of v0, /device:TPU:1, one launch (start us, length us, event | category | flops | bytes accessed | tf_op | source)
XLA Modules:
  0.0 307.8 jit_solution(14724975885736214320)
XLA Ops:
  7.2 0.0 copy-start
  7.2 0.0 all-gather.2.cloned.1.call-start
  7.2 0.8 eq.29
  8.1 0.8 reshape.271
  8.8 0.1 fusion.20
  8.9 0.1 reduce_window_sum.11
  9.0 0.2 select_reduce_fusion
  9.2 0.8 scatter_custom_fusion
  10.0 1.1 fusion.16
  11.1 1.0 scatter_custom_fusion.1
  12.1 0.1 mul.76
  12.2 1.0 fusion.18
  13.2 1.7 gather_fusion
  14.9 0.2 copy_multiply_fusion
  15.1 48.6 %all_to_all.10 = bf16[2,8,8,7168]{3,2,0,1:T(8,128)(2,1)S(1)} all-to-all(bf16[2,8,8,7168]{3,2,0,1:T(8,128)(2,1)S(1)} %copy_multiply_fusion), channel_id=1, replica_groups=mesh['rep'=4,'ep'=8] {'ep'}, dimensions={1} | all-to-all | bytes 3670016 | tf_op jit(solution)/shard_map/all_to_all | solution.py:64
  63.7 1.5 copy.29
  65.1 0.0 all-gather.2.cloned.1.call-update
  65.2 0.0 reduce-scatter.2.cloned.1.call-start
  65.2 78.3 %all-gather.2.cloned.1.call-done = bf16[2,256,7168]{2,1,0:T(8,128)(2,1)} async-done(((bf16[2,64,7168]{2,1,0:T(8,128)(2,1)}), bf16[2,256,7168]{2,1,0:T(8,128)(2,1)}) %all-gather.2.cloned.1.call-update) | async-done | bytes 7340048 | tf_op jit(solution)/shard_map/all_gather | solution.py:80
  143.5 7.2 %fusion.34 = f32[2,256,256]{2,1,0:T(8,128)S(1)} fusion(bf16[2,256,7168]{2,1,0:T(8,128)(2,1)} %all-gather.2.cloned.1.call-done, bf16[2,7168,256]{2,1,0:T(8,128)(2,1)} %param.21), kind=kOutput, calls=%fused_computation.66 | convolution fusion | flops 1879048192 | bytes 15204352 | tf_op jit(solution)/shard_map/vmap()/dot_general | solution.py:23
  150.7 14.3 %convolution_convert_fusion = bf16[2,256,7168]{2,1,0:T(8,128)(2,1)} fusion(bf16[2,256,7168]{2,1,0:T(8,128)(2,1)} %param.23, bf16[2,256,7168]{2,1,0:T(8,128)(2,1)} %all-gather.2.cloned.1.call-done, bf16[2,7168,256]{2,1,0:T(8,128)(2,1)} %param.22, f32[2,256,256]{2,1,0:T(8,128)S(1)} %fusion.34), kind=kOutput, calls=%fused_computation.5 | convolution fusion | flops 3762552832 | bytes 29884416 | tf_op jit(solution)/shard_map/vmap()/dot_general | solution.py:26
  165.0 0.0 copy-start.6
  165.0 0.0 copy-start.1
  165.0 0.0 copy-start.3
  165.1 0.0 copy-start.4
  165.1 0.0 reduce-scatter.2.cloned.1.call-update
  165.1 79.1 %reduce-scatter.2.cloned.1.call-done = bf16[2,64,7168]{2,1,0:T(8,128)(2,1)} async-done(((bf16[2,256,7168]{2,1,0:T(8,128)(2,1)}), bf16[2,64,7168]{2,1,0:T(8,128)(2,1)}) %reduce-scatter.2.cloned.1.call-update) | async-done | bytes 1835024 | tf_op jit(solution)/shard_map/reduce_scatter | solution.py:83
  244.2 2.8 copy.19
  247.0 5.3 %all-to-all-start.1 = ((bf16[2,8,8,7168]{3,2,0,1:T(8,128)(2,1)}), bf16[2,8,8,7168]{3,2,0,1:T(8,128)(2,1)}, u32[]{:S(2)}, u32[]{:S(2)}) async-start(bf16[2,8,8,7168]{3,2,0,1:T(8,128)(2,1)} %copy.19), calls=%async_computation.2 | async-start | bytes 3670016 | tf_op jit(solution)/shard_map/all_to_all | solution.py:86
  252.3 0.0 copy-done.6
  252.3 0.1 iota_compare_fusion.1
  252.4 0.0 copy-done
  252.4 0.0 copy-done.1
  252.4 0.4 fusion.33
  252.8 0.0 copy-done.3
  252.9 0.0 copy-done.4
  252.9 0.3 fusion.5
  253.2 0.2 fusion.32
  253.4 0.0 copy-start.5
  253.4 1.7 convolution_convert_fusion.1
  255.1 0.0 copy-start.2
  255.1 39.9 %all-to-all-done.1 = bf16[2,8,8,7168]{3,2,0,1:T(8,128)(2,1)} async-done(((bf16[2,8,8,7168]{3,2,0,1:T(8,128)(2,1)}), bf16[2,8,8,7168]{3,2,0,1:T(8,128)(2,1)}, u32[]{:S(2)}, u32[]{:S(2)}) %all-to-all-start.1) | async-done | bytes 1835040 | tf_op jit(solution)/shard_map/all_to_all | solution.py:86
  295.0 1.6 copy.20
  296.6 2.1 gather_fusion.1
  298.7 0.0 copy-done.5
  298.7 1.6 fusion.7
  300.2 0.0 copy-done.2
  300.3 0.7 fusion.19
  (8 shorter events, 0.1 us)
Async XLA Ops:
  7.2 245.2 %copy-start = (bf16[8,128,512]{2,1,0:T(8,128)(2,1)S(1)}, bf16[8,128,512]{2,1,0:T(8,128)(2,1)}, u32[]{:S(2)}) copy-start(bf16[8,128,512]{2,1,0:T(8,128)(2,1)} %param.14) | copy-start | bytes 3145732
  7.2 136.3 %all-gather.2.cloned.1.call-start = ((), (), s32[]{:S(2)}) async-start(), calls=%async_computation.3 | async-start | bytes 9175040 | tf_op jit(solution)/shard_map/all_gather | solution.py:80
  65.2 179.0 %reduce-scatter.2.cloned.1.call-start = ((), (), s32[]{:S(2)}) async-start(), calls=%async_computation.4 | async-start | bytes 9175040 | tf_op jit(solution)/shard_map/reduce_scatter | solution.py:83
  165.0 87.3 %copy-start.6 = (s32[8]{0:T(128)S(1)}, s32[8]{0:T(128)}, u32[]{:S(2)}) copy-start(s32[8]{0:T(128)} %param.16) | copy-start | bytes 100
  165.0 87.4 %copy-start.1 = (bf16[8,128,512]{2,1,0:T(8,128)(2,1)S(1)}, bf16[8,128,512]{2,1,0:T(8,128)(2,1)}, u32[]{:S(2)}) copy-start(bf16[8,128,512]{2,1,0:T(8,128)(2,1)} %param.12) | copy-start | bytes 3145732
  165.0 87.8 %copy-start.3 = (bf16[8,128,64]{1,2,0:T(8,128)(2,1)S(1)}, bf16[8,128,64]{1,2,0:T(8,128)(2,1)}, u32[]{:S(2)}) copy-start(bf16[8,128,64]{1,2,0:T(8,128)(2,1)} %param.13) | copy-start | bytes 393220
  165.1 87.8 %copy-start.4 = (bf16[8,128,64]{1,2,0:T(8,128)(2,1)S(1)}, bf16[8,128,64]{1,2,0:T(8,128)(2,1)}, u32[]{:S(2)}) copy-start(bf16[8,128,64]{1,2,0:T(8,128)(2,1)} %param.15) | copy-start | bytes 393220
  247.0 48.0 %all-to-all-start.1 = ((bf16[2,8,8,7168]{3,2,0,1:T(8,128)(2,1)}), bf16[2,8,8,7168]{3,2,0,1:T(8,128)(2,1)}, u32[]{:S(2)}, u32[]{:S(2)}) async-start(bf16[2,8,8,7168]{3,2,0,1:T(8,128)(2,1)} %copy.19), calls=%async_computation.2 | async-start | bytes 3670016 | tf_op jit(solution)/shard_map/all_to_all | solution.py:86
  253.4 45.3 %copy-start.5 = (bf16[8,8]{1,0:T(8,128)(2,1)S(1)}, bf16[8,8]{1,0:T(8,128)(2,1)}, u32[]{:S(2)}) copy-start(bf16[8,8]{1,0:T(8,128)(2,1)} %param.20) | copy-start | bytes 388
  255.1 45.1 %copy-start.2 = (bf16[8,7168]{1,0:T(8,128)(2,1)S(1)}, bf16[8,7168]{1,0:T(8,128)(2,1)}, u32[]{:S(2)}) copy-start(bf16[8,7168]{1,0:T(8,128)(2,1)} %param.17) | copy-start | bytes 344068
Sparse Core Ops, SparseCore 0:
  65.3 78.1 all-gather.1
  165.2 78.9 reduce-scatter.1
where the time goes:
time: 309 us; the launch traced here: 308 us
  waiting for transfers between devices  197 us (64%)
  blocking collectives  48.6 us (16%)
  matrix products  25.5 us (8%)
  between operations  14.2 us (5%)
  local copies, waits for them, and re-layouts  13.1 us (4%)
  starting transfers between devices  5.35 us (2%)
  other arithmetic  3.63 us (1%)
    reduce_scatter x1, waiting for transfers between devices, per_device(): lax.psum_scatter(partials.astype(jnp.float32).astype(jnp.bfloat16), 'rep'...  79.1 us
    all_gather x1, waiting for transfers between devices, per_device(): everyone = lax.all_gather(incoming, 'rep', axis=1, tiled=True)  78.3 us
    all_to_all x1, blocking collectives, per_device(): lax.all_to_all(outgoing, 'ep', split_axis=1, concat_axis=1, tiled=True)  48.6 us
    all_to_all x1, waiting for transfers between devices, per_device(): lax.all_to_all(summed.reshape(local_count, ep_count, capacity, feature_di...  39.9 us
    dot_general x1, matrix products, expert_block(): jnp.dot(hidden, down_part, preferred_element_type=jnp.float32)  14.3 us
    dot_general x1, matrix products, expert_block(): gate_act = jnp.dot(tokens_in, gate_part, preferred_element_type=jnp.float32)  7.22 us
  transfers between devices with their start and end apart: 3, of which 3 were waited for; matrix products, arithmetic and copies ran while one was open for 1% of the time, Pallas kernels for 0%

commit v1 on v0

--- a/solution.py
+++ b/solution.py
@@ -1,16 +1,24 @@
+import functools
+
 import jax
 import jax.numpy as jnp
 from jax import lax
+from jax.experimental import pallas as pl
+from jax.experimental.pallas import tpu as pltpu
 from jax.sharding import PartitionSpec as P
+
+MESH = pl.DeviceIdType.MESH
+LANES = 128
+PARTS = 7
 
 score_scale = 192.0 ** (-0.5)
 norm_eps = 1e-06
 
 
-def slot_ranks(route_table, expert_total):
-    onehot = (route_table[..., None] == jnp.arange(expert_total, dtype=jnp.int32)).astype(jnp.int32)
-    earlier = jnp.cumsum(onehot, axis=1) - onehot
-    return jnp.sum(earlier * onehot, axis=-1)
+def slot_ranks(routes):
+    order = jnp.arange(routes.shape[0], dtype=jnp.int32)
+    earlier = (routes[:, None] == routes[None, :]) & (order[None, :] < order[:, None])
+    return jnp.sum(earlier.astype(jnp.int32), axis=-1)
 
 
 def fill_slots(features, slot_index, row_index, slot_total):
@@ -53,7 +61,7 @@
         * norm_gain
     ).astype(jnp.bfloat16)
     flat_routes = expert_ids.reshape(-1)
-    rank_in = slot_ranks(flat_routes.reshape(1, -1), expert_total)[0]
+    rank_in = slot_ranks(flat_routes)
     expert_slot = flat_routes % local_count * ep_count + flat_routes // local_count
     slot_index = expert_slot * capacity + rank_in
     row_index = jnp.arange(row_count * top_count, dtype=jnp.int32) // top_count
@@ -100,6 +108,309 @@
     return (attn_latent, layer_out)
 
 
+def fused_kernel(
+    parts,
+    ql_hbm, qr_hbm, cl_hbm, cr_hbm, len_ref, stream_ref, gain_ref, ids_ref, rw_ref,
+    wg_hbm, wu_hbm, wd_hbm,
+    attn_hbm, out_ref,
+    ql, qr, cl, cr, attn, wg, wu, wd,
+    nrm, swap_out, swap_in, xs, table, acc, hid,
+    ysib, yown, r1, zb, ra, rb, rc, fin, fin_in,
+    load_sem, w_sem, swap_sem,
+    gz_s, gz_r, gc_s, gc_r, gf_s, gf_r, gs_s, gs_r,
+    r1_s, r1_r, ra_s, ra_r, rb_s, rb_r, rc_s, rc_r, fin_s, fin_r,
+):
+    rep = lax.axis_index("rep")
+    ep = lax.axis_index("ep")
+    z, c = ep // 2, ep % 2
+    other = 1 - c
+    xn = rep + 1 - 2 * (rep % 2)
+    yn = (rep + 2) % 4
+    dg = 3 - rep
+    sib_id = (rep, z * 2 + other)
+    x_id, y_id = (xn, ep), (yn, ep)
+
+    def z_id(d):
+        return (rep, ((z + d) % 4) * 2 + c)
+
+    partners = [sib_id, x_id, y_id, z_id(1), z_id(2), z_id(3)]
+    rows, width = stream_ref.shape
+    half = width // 2
+    chunk = half // parts
+    local = wg.shape[0]
+    ff = wg.shape[2]
+    total = 32 * rows
+
+    barrier = pltpu.get_barrier_semaphore()
+    for p in partners:
+        pl.semaphore_signal(barrier, inc=1, device_id=p, device_id_type=MESH)
+
+    loads = []
+    for n, (a, b) in enumerate([(ql_hbm, ql), (cl_hbm, cl), (qr_hbm, qr), (cr_hbm, cr)]):
+        loads.append(pltpu.make_async_copy(a, b, load_sem.at[n]))
+    weights = []
+    for e in range(local):
+        weights.append(pltpu.make_async_copy(wg_hbm.at[e], wg.at[e], w_sem.at[3 * e]))
+        weights.append(pltpu.make_async_copy(wu_hbm.at[e], wu.at[e], w_sem.at[3 * e + 1]))
+        weights.append(
+            pltpu.make_async_copy(wd_hbm.at[e], wd.at[pl.ds(e * ff, ff)], w_sem.at[3 * e + 2])
+        )
+    for copy in loads + weights:
+        copy.start()
+
+    stream_f = stream_ref[...].astype(jnp.float32)
+    scale = lax.rsqrt(jnp.mean(stream_f * stream_f, axis=-1, keepdims=True) + norm_eps)
+    normed = (stream_f * scale * gain_ref[...]).astype(jnp.bfloat16).astype(jnp.float32)
+    for h in range(2):
+        nrm[h, :, :half] = normed[:, h * half : (h + 1) * half]
+    lane = lax.broadcasted_iota(jnp.int32, (rows, LANES), 1)
+    dense = jnp.zeros((rows, LANES), jnp.float32)
+    ids, rw = ids_ref[...], rw_ref[...].astype(jnp.float32)
+    for k in range(ids.shape[1]):
+        dense = dense + jnp.where(lane == ids[:, k : k + 1], rw[:, k : k + 1], 0.0)
+    for h in range(2):
+        nrm[h, :, half:] = dense
+    swap_out[...] = nrm[other]
+    pl.semaphore_wait(barrier, len(partners))
+
+    sent = []
+
+    def send(src, dst, send_sem, recv_sem, to):
+        copy = pltpu.make_async_remote_copy(
+            src_ref=src, dst_ref=dst, send_sem=send_sem, recv_sem=recv_sem,
+            device_id=to, device_id_type=MESH,
+        )
+        copy.start()
+        sent.append(copy)
+
+    def arrived(dst, send_sem, recv_sem, to):
+        pltpu.make_async_remote_copy(
+            src_ref=dst, dst_ref=dst, send_sem=send_sem, recv_sem=recv_sem,
+            device_id=to, device_id_type=MESH,
+        ).wait_recv()
+
+    send(swap_out, swap_in, swap_sem.at[0], swap_sem.at[1], sib_id)
+    arrived(swap_in, swap_sem.at[0], swap_sem.at[1], sib_id)
+    mine, theirs = nrm[c], swap_in[...]
+    both = jnp.where(
+        c == 0,
+        jnp.concatenate([mine, theirs], axis=0),
+        jnp.concatenate([theirs, mine], axis=0),
+    ).astype(jnp.bfloat16)
+    table[rep, z] = both[:, half:]
+    units = [table]
+    for k in range(parts):
+        xs[c * parts + k, rep, z] = both[:, k * chunk : (k + 1) * chunk]
+        units.append(xs.at[c * parts + k])
+
+    def gather_z(u):
+        for d in (1, 2, 3):
+            blk = units[u].at[rep, z]
+            send(blk, blk, gz_s.at[u, d - 1], gz_r.at[u, d - 1], z_id(d))
+
+    def gather_xy(u):
+        for d in (1, 2, 3):
+            blk = units[u].at[rep, (z + 4 - d) % 4]
+            arrived(blk, gz_s.at[u, d - 1], gz_r.at[u, d - 1], z_id(4 - d))
+        col = units[u].at[rep]
+        send(col, col, gc_s.at[u, 0], gc_r.at[u, 0], x_id)
+        send(col, col, gc_s.at[u, 1], gc_r.at[u, 1], y_id)
+
+    def gather_diag(u):
+        arrived(units[u].at[xn], gc_s.at[u, 0], gc_r.at[u, 0], x_id)
+        low = units[u].at[xn, pl.ds(0, 2)]
+        send(low, low, gf_s.at[u, 0], gf_r.at[u, 0], y_id)
+        arrived(units[u].at[yn], gc_s.at[u, 1], gc_r.at[u, 1], y_id)
+        high = units[u].at[yn, pl.ds(2, 2)]
+        send(high, high, gf_s.at[u, 1], gf_r.at[u, 1], x_id)
+
+    def gather_done(u):
+        arrived(units[u].at[dg, pl.ds(0, 2)], gf_s.at[u, 0], gf_r.at[u, 0], y_id)
+        arrived(units[u].at[dg, pl.ds(2, 2)], gf_s.at[u, 1], gf_r.at[u, 1], x_id)
+        if u > 0:
+            send(units[u], units[u], gs_s.at[u - 1], gs_r.at[u - 1], sib_id)
+
+    def attend(i):
+        dims = (((1,), (1,)), ((), ()))
+        s = lax.dot_general(ql[i], cl[i], dims, preferred_element_type=jnp.float32)
+        s = s + lax.dot_general(qr[i], cr[i], dims, preferred_element_type=jnp.float32)
+        s = s * score_scale
+        live = lax.broadcasted_iota(jnp.int32, s.shape, 1) < len_ref[i]
+        s = jnp.where(live, s, -1e30)
+        top = jnp.max(s, axis=-1, keepdims=True)
+        w = jnp.where(live, jnp.exp(s - top), 0.0)
+        w = (w / jnp.sum(w, axis=-1, keepdims=True)).astype(jnp.bfloat16)
+        attn[i] = jnp.dot(w, cl[i], preferred_element_type=jnp.float32).astype(jnp.bfloat16)
+
+    def project(g, first):
+        x = xs[g].reshape(total, chunk)
+        at = pl.ds(pl.multiple_of(g * chunk, chunk), chunk)
+        for e in range(local):
+            for n, w in enumerate((wg, wu)):
+                y = jnp.dot(x, w[e, at, :], preferred_element_type=jnp.float32)
+                if first:
+                    acc[2 * e + n] = y
+                else:
+                    acc[2 * e + n] = acc[2 * e + n] + y
+
+    for u in range(parts + 1):
+        gather_z(u)
+    for copy in loads:
+        copy.wait()
+    attend(0)
+    attended = 1
+    attn_copy = None
+    waited = False
+    for t in range(parts + 4):
+        if t <= parts:
+            gather_xy(t)
+        if 0 <= t - 1 <= parts:
+            gather_diag(t - 1)
+        if 0 <= t - 2 <= parts:
+            gather_done(t - 2)
+        while attended < rows and (attended <= t + 1 or t >= 2):
+            attend(attended)
+            attended += 1
+            if t < parts + 1:
+                break
+        if attended == rows and attn_copy is None:
+            attn_copy = pltpu.make_async_copy(attn, attn_hbm, load_sem.at[4])
+            attn_copy.start()
+        if not waited and t >= 3:
+            for copy in weights:
+                copy.wait()
+            waited = True
+        if 1 <= t - 2 <= parts:
+            k = t - 3
+            if waited:
+                project(c * parts + k, k == 0)
+        if 1 <= t - 3 <= parts:
+            k = t - 4
+            g = other * parts + k
+            arrived(xs.at[g], gs_s.at[k], gs_r.at[k], sib_id)
+            project(g, False)
+
+    col = lax.broadcasted_iota(jnp.int32, (total, LANES), 1)
+    routes = table[...].reshape(total, LANES).astype(jnp.float32)
+    for e in range(local):
+        w = jnp.sum(jnp.where(col == ep * local + e, routes, 0.0), axis=-1, keepdims=True)
+        gate, up = acc[2 * e], acc[2 * e + 1]
+        hid[:, e * ff : (e + 1) * ff] = (gate / (1.0 + jnp.exp(-gate)) * up * w).astype(
+            jnp.bfloat16
+        )
+
+    def f32(v):
+        return v.astype(jnp.float32)
+
+    def down(k):
+        for own in (False, True):
+            g = (c if own else other) * parts + k
+            at = pl.ds(pl.multiple_of(g * chunk, chunk), chunk)
+            y = jnp.dot(hid[...], wd[:, at], preferred_element_type=jnp.float32)
+            if own:
+                yown[k] = y.reshape(yown.shape[1:])
+            else:
+                ysib[k] = y.astype(jnp.bfloat16).reshape(ysib.shape[1:])
+                send(ysib.at[k], r1.at[k], r1_s.at[k], r1_r.at[k], sib_id)
+
+    def reduce_pair(k):
+        arrived(r1.at[k], r1_s.at[k], r1_r.at[k], sib_id)
+        zb[k] = (yown[k] + f32(r1[k])).astype(jnp.bfloat16)
+        send(zb.at[k, dg, pl.ds(0, 2)], ra.at[k, 0], ra_s.at[k, 0], ra_r.at[k, 0], x_id)
+        send(zb.at[k, dg, pl.ds(2, 2)], ra.at[k, 1], ra_s.at[k, 1], ra_r.at[k, 1], y_id)
+
+    def reduce_diag(k):
+        arrived(ra.at[k, 0], ra_s.at[k, 0], ra_r.at[k, 0], x_id)
+        zb[k, yn, 0:2] = (f32(zb[k, yn, 0:2]) + f32(ra[k, 0])).astype(jnp.bfloat16)
+        send(zb.at[k, yn], rb.at[k, 1], rb_s.at[k, 1], rb_r.at[k, 1], y_id)
+        arrived(ra.at[k, 1], ra_s.at[k, 1], ra_r.at[k, 1], y_id)
+        zb[k, xn, 2:4] = (f32(zb[k, xn, 2:4]) + f32(ra[k, 1])).astype(jnp.bfloat16)
+        send(zb.at[k, xn], rb.at[k, 0], rb_s.at[k, 0], rb_r.at[k, 0], x_id)
+
+    def reduce_xy(k):
+        arrived(rb.at[k, 1], rb_s.at[k, 1], rb_r.at[k, 1], y_id)
+        arrived(rb.at[k, 0], rb_s.at[k, 0], rb_r.at[k, 0], x_id)
+        zb[k, rep] = (f32(zb[k, rep]) + f32(rb[k, 0]) + f32(rb[k, 1])).astype(jnp.bfloat16)
+        for d in (1, 2, 3):
+            send(
+                zb.at[k, rep, (z + d) % 4], rc.at[k, d - 1],
+                rc_s.at[k, d - 1], rc_r.at[k, d - 1], z_id(d),
+            )
+
+    def reduce_z(k):
+        s = f32(zb[k, rep, z])
+        for d in (1, 2, 3):
+            arrived(rc.at[k, d - 1], rc_s.at[k, d - 1], rc_r.at[k, d - 1], z_id(4 - d))
+            s = s + f32(rc[k, d - 1])
+        fin[k] = s.reshape(2, rows, chunk)
+        send(fin.at[k, other], fin_in.at[k], fin_s.at[k], fin_r.at[k], sib_id)
+
+    def finish(k):
+        arrived(fin_in.at[k], fin_s.at[k], fin_r.at[k], sib_id)
+        mine, theirs = fin[k, c], fin_in[k]
+        for h in range(2):
+            at = slice(h * half + k * chunk, h * half + (k + 1) * chunk)
+            out_ref[:, at] = (
+                f32(stream_ref[:, at]) + jnp.where(c == h, mine, theirs)
+            ).astype(jnp.bfloat16)
+
+    stages = [down, reduce_pair, reduce_diag, reduce_xy, reduce_z, finish]
+    for t in range(parts + len(stages) - 1):
+        for n, stage in enumerate(stages):
+            if 0 <= t - n < parts:
+                stage(t - n)
+    for copy in sent:
+        copy.wait_send()
+    attn_copy.wait()
+
+
+def fused(parts, *args):
+    (q_latent, q_rope, cache_latent, cache_rope, cache_len, stream, norm_gain,
+     expert_ids, route_weights, w_gate, w_up, w_down) = args
+    rows, width = stream.shape
+    half = width // 2
+    chunk = half // parts
+    local, _, ff = w_gate.shape
+    total = 32 * rows
+    pair = 2 * rows
+    bf, fl = jnp.bfloat16, jnp.float32
+    vm, dma = pltpu.VMEM, pltpu.SemaphoreType.DMA
+    space = lambda s: pl.BlockSpec(memory_space=s)
+    in_specs = [space(pl.ANY)] * 4 + [space(pltpu.SMEM)] + [space(vm)] * 4 + [space(pl.ANY)] * 3
+    scratch = [
+        vm(q_latent.shape, bf), vm(q_rope.shape, bf), vm(cache_latent.shape, bf),
+        vm(cache_rope.shape, bf), vm(q_latent.shape, bf),
+        vm(w_gate.shape, bf), vm(w_up.shape, bf), vm((local * ff, width), bf),
+        vm((2, rows, half + LANES), fl), vm((rows, half + LANES), fl), vm((rows, half + LANES), fl),
+        vm((2 * parts, 4, 4, pair, chunk), bf), vm((4, 4, pair, LANES), bf),
+        vm((2 * local, total, ff), fl), vm((total, local * ff), bf),
+        vm((parts, 4, 4, pair, chunk), bf), vm((parts, 4, 4, pair, chunk), fl),
+        vm((parts, 4, 4, pair, chunk), bf), vm((parts, 4, 4, pair, chunk), bf),
+        vm((parts, 2, 2, pair, chunk), bf), vm((parts, 2, 4, pair, chunk), bf),
+        vm((parts, 3, pair, chunk), bf), vm((parts, 2, rows, chunk), fl), vm((parts, rows, chunk), fl),
+        dma((5,)), dma((3 * local,)), dma((2,)),
+        dma((parts + 1, 3)), dma((parts + 1, 3)), dma((parts + 1, 2)), dma((parts + 1, 2)),
+        dma((parts + 1, 2)), dma((parts + 1, 2)), dma((parts,)), dma((parts,)),
+        dma((parts,)), dma((parts,)), dma((parts, 2)), dma((parts, 2)),
+        dma((parts, 2)), dma((parts, 2)), dma((parts, 3)), dma((parts, 3)),
+        dma((parts,)), dma((parts,)),
+    ]
+    return pl.pallas_call(
+        functools.partial(fused_kernel, parts),
+        out_shape=(
+            jax.ShapeDtypeStruct(q_latent.shape, bf),
+            jax.ShapeDtypeStruct(stream.shape, bf),
+        ),
+        in_specs=in_specs,
+        out_specs=(space(pl.ANY), space(vm)),
+        scratch_shapes=scratch,
+        compiler_params=pltpu.CompilerParams(
+            collective_id=0, has_side_effects=True, vmem_limit_bytes=58 * 2**20
+        ),
+    )(q_latent, q_rope, cache_latent, cache_rope, cache_len, stream,
+      norm_gain.reshape(1, width), expert_ids, route_weights, w_gate, w_up, w_down)
+
+
 def solution(mesh):
     placed = (
         P(("rep", "ep"), None, None),
@@ -115,8 +426,9 @@
         P("ep", None, "rep"),
         P("ep", "rep", None),
     )
+    small = mesh.shape["rep"] == 4 and mesh.shape["ep"] == 8
     return jax.shard_map(
-        per_device,
+        functools.partial(fused, PARTS) if small else per_device,
         mesh=mesh,
         in_specs=placed,
         out_specs=(P(("rep", "ep"), None, None), P(("rep", "ep"), None)),

time: 309 us -> 77 us (0.25)
  waiting for transfers between devices: 197 us -> 0 us
  Pallas kernels: 0 us -> 68.9 us
  blocking collectives: 48.6 us -> 0 us
  matrix products: 25.5 us -> 0 us
  between operations: 14.2 us -> 0.64 us
  local copies, waits for them, and re-layouts: 13.1 us -> 7.31 us
  starting transfers between devices: 5.35 us -> 0 us
  other arithmetic: 3.63 us -> 0 us
    reduce_scatter x1 -> x0, waiting for transfers between devices: 79.1 us -> none  [per_device(): lax.psum_scatter(partials.astype(jnp.float32).astype(jnp.bfloat16), 'rep'...]
    all_gather x1 -> x0, waiting for transfers between devices: 78.3 us -> none  [per_device(): everyone = lax.all_gather(incoming, 'rep', axis=1, tiled=True)]
    pallas_call x0 -> x1, Pallas kernels: none -> 68.9 us  [fused(): pl.pallas_call(functools.partial(fused_kernel, parts), out_shape=(jax.Sha...]
    all_to_all x1 -> x0, blocking collectives: 48.6 us -> none  [per_device(): lax.all_to_all(outgoing, 'ep', split_axis=1, concat_axis=1, tiled=True)]
    all_to_all x1 -> x0, waiting for transfers between devices: 39.9 us -> none  [per_device(): lax.all_to_all(summed.reshape(local_count, ep_count, capacity, feature_di...]
    dot_general x6 -> x0, matrix products: 25.5 us -> none  [the longest x1 14.3 us: expert_block(): jnp.dot(hidden, down_part, preferred_element_type=jnp.float32)]
    unnamed x14 -> x4, local copies, waits for them, and re-layouts: 0.03 us -> 7.31 us
    all_to_all x1 -> x0, starting transfers between devices: 5.27 us -> none  [per_device(): lax.all_to_all(summed.reshape(local_count, ep_count, capacity, feature_di...]
  transfers between devices with their start and end apart: 3 -> 0, of which waited for: 3 -> 0; matrix products, arithmetic and copies ran while one was open for 1% -> 0% of each run, Pallas kernels for 0% -> 0%
where the time goes in v1:
time: 77 us; the launch traced here: 76.8 us
  Pallas kernels  68.9 us (89%)
  local copies, waits for them, and re-layouts  7.31 us (9%)
    pallas_call x1, Pallas kernels, fused(): pl.pallas_call(functools.partial(fused_kernel, parts), out_shape=(jax.Sha...  68.9 us
    unnamed x4, local copies, waits for them, and re-layouts  7.31 us

profile of v1, /device:TPU:1, one launch (start us, length us, event | category | flops | bytes accessed | tf_op | source)
XLA Modules:
  0.0 76.8 jit_solution(2583628322041673169)
XLA Ops:
  0.6 1.7 %copy.14.qr_hbm = bf16[8,128,64]{2,1,0:T(8,128)(2,1)} copy(bf16[8,128,64]{1,2,0:T(8,128)(2,1)} %param.13) | data formatting | bytes 262144 | tf_op args[1]
  2.4 1.7 %copy.15.cr_hbm = bf16[8,128,64]{2,1,0:T(8,128)(2,1)} copy(bf16[8,128,64]{1,2,0:T(8,128)(2,1)} %param.15) | data formatting | bytes 262144 | tf_op args[3]
  4.1 68.9 %shard_map.131 = (bf16[8,128,512]{2,1,0:T(8,128)(2,1)}, bf16[8,7168]{1,0:T(8,128)(2,1)}) custom-call(bf16[8,128,512]{2,1,0:T(8,128)(2,1)} %ql_hbm.1, bf16[8,128,64]{2,1,0:T(8,128)(2,1)} %copy.14.qr_hbm, bf16[8,128,512]{2,1,0:T(8,128)(2,1)} %cl_hbm.1, bf16[8,128,64]{2,1,0:T(8,128)(2,1)} %copy.15.cr_hbm, s32[8]{0:T(128)} %len_ref.1, ...), custom_call_target="tpu_custom_call" | custom-call | tf_op jit(solution)/shard_map/pallas_call | solution.py:398
  73.0 2.3 %copy.18 = bf16[8,128,512]{2,1,0:T(8,128)(2,1)} copy(bf16[8,128,512]{2,1,0:T(8,128)(2,1)} %get-tuple-element.4) | data formatting | bytes 2097152
  75.3 1.6 %copy.19 = bf16[8,7168]{1,0:T(8,128)(2,1)} copy(bf16[8,7168]{1,0:T(8,128)(2,1)} %get-tuple-element.5) | data formatting | bytes 229376

commit v2 on v1

--- a/solution.py
+++ b/solution.py
@@ -9,7 +9,7 @@
 
 MESH = pl.DeviceIdType.MESH
 LANES = 128
-PARTS = 7
+PARTS = 4
 
 score_scale = 192.0 ** (-0.5)
 norm_eps = 1e-06
@@ -116,7 +116,7 @@
     ql, qr, cl, cr, attn, wg, wu, wd,
     nrm, swap_out, swap_in, xs, table, acc, hid,
     ysib, yown, r1, zb, ra, rb, rc, fin, fin_in,
-    load_sem, w_sem, swap_sem,
+    load_sem, w_sem, swap_sem, go_s, go_r,
     gz_s, gz_r, gc_s, gc_r, gf_s, gf_r, gs_s, gs_r,
     r1_s, r1_r, ra_s, ra_r, rb_s, rb_r, rc_s, rc_r, fin_s, fin_r,
 ):
@@ -198,10 +198,16 @@
         jnp.concatenate([theirs, mine], axis=0),
     ).astype(jnp.bfloat16)
     table[rep, z] = both[:, half:]
-    units = [table]
+    units = []
     for k in range(parts):
         xs[c * parts + k, rep, z] = both[:, k * chunk : (k + 1) * chunk]
         units.append(xs.at[c * parts + k])
+    units.append(table)
+    own = pl.ds(c * parts, parts)
+    for n, to in enumerate((x_id, y_id)):
+        send(xs.at[own, rep, z], xs.at[own, rep, z], go_s.at[n], go_r.at[n], to)
+        blk = table.at[rep, z]
+        send(blk, blk, go_s.at[n + 2], go_r.at[n + 2], to)
 
     def gather_z(u):
         for d in (1, 2, 3):
@@ -212,28 +218,38 @@
         for d in (1, 2, 3):
             blk = units[u].at[rep, (z + 4 - d) % 4]
             arrived(blk, gz_s.at[u, d - 1], gz_r.at[u, d - 1], z_id(4 - d))
-        col = units[u].at[rep]
-        send(col, col, gc_s.at[u, 0], gc_r.at[u, 0], x_id)
-        send(col, col, gc_s.at[u, 1], gc_r.at[u, 1], y_id)
+            send(blk, blk, gc_s.at[u, d - 1], gc_r.at[u, d - 1], x_id)
+            send(blk, blk, gc_s.at[u, d + 2], gc_r.at[u, d + 2], y_id)
+
+    def column_in(u, n, src, to):
+        if u == 0:
+            arrived(xs.at[own, src, z], go_s.at[n], go_r.at[n], to)
+        if u == parts:
+            arrived(table.at[src, z], go_s.at[n + 2], go_r.at[n + 2], to)
+        for d in (1, 2, 3):
+            m = d - 1 + 3 * n
+            arrived(units[u].at[src, (z + 4 - d) % 4], gc_s.at[u, m], gc_r.at[u, m], to)
 
     def gather_diag(u):
-        arrived(units[u].at[xn], gc_s.at[u, 0], gc_r.at[u, 0], x_id)
+        column_in(u, 0, xn, x_id)
         low = units[u].at[xn, pl.ds(0, 2)]
         send(low, low, gf_s.at[u, 0], gf_r.at[u, 0], y_id)
-        arrived(units[u].at[yn], gc_s.at[u, 1], gc_r.at[u, 1], y_id)
+        column_in(u, 1, yn, y_id)
         high = units[u].at[yn, pl.ds(2, 2)]
         send(high, high, gf_s.at[u, 1], gf_r.at[u, 1], x_id)
 
     def gather_done(u):
         arrived(units[u].at[dg, pl.ds(0, 2)], gf_s.at[u, 0], gf_r.at[u, 0], y_id)
         arrived(units[u].at[dg, pl.ds(2, 2)], gf_s.at[u, 1], gf_r.at[u, 1], x_id)
-        if u > 0:
-            send(units[u], units[u], gs_s.at[u - 1], gs_r.at[u - 1], sib_id)
+        if u < parts:
+            send(units[u], units[u], gs_s.at[u], gs_r.at[u], sib_id)
 
     def attend(i):
         dims = (((1,), (1,)), ((), ()))
         s = lax.dot_general(ql[i], cl[i], dims, preferred_element_type=jnp.float32)
-        s = s + lax.dot_general(qr[i], cr[i], dims, preferred_element_type=jnp.float32)
+        s = s + lax.dot_general(
+            qr[i], cr[i], (((0,), (0,)), ((), ())), preferred_element_type=jnp.float32
+        )
         s = s * score_scale
         live = lax.broadcasted_iota(jnp.int32, s.shape, 1) < len_ref[i]
         s = jnp.where(live, s, -1e30)
@@ -253,39 +269,37 @@
                 else:
                     acc[2 * e + n] = acc[2 * e + n] + y
 
-    for u in range(parts + 1):
-        gather_z(u)
+    def step(stage, u):
+        if 0 <= u < parts:
+            stage(u)
+        if u == 0:
+            stage(parts)
+
+    for u in range(parts):
+        step(gather_z, u)
     for copy in loads:
         copy.wait()
     attend(0)
+    step(gather_xy, 0)
+    step(gather_xy, 1)
     attended = 1
-    attn_copy = None
-    waited = False
-    for t in range(parts + 4):
-        if t <= parts:
-            gather_xy(t)
-        if 0 <= t - 1 <= parts:
-            gather_diag(t - 1)
-        if 0 <= t - 2 <= parts:
-            gather_done(t - 2)
-        while attended < rows and (attended <= t + 1 or t >= 2):
+    for t in range(parts + 3):
+        step(gather_xy, t + 2)
+        step(gather_diag, t)
+        step(gather_done, t - 1)
+        while attended < rows and (attended <= t + 1 or t == parts + 2):
             attend(attended)
             attended += 1
-            if t < parts + 1:
-                break
-        if attended == rows and attn_copy is None:
+        if t == parts + 2:
             attn_copy = pltpu.make_async_copy(attn, attn_hbm, load_sem.at[4])
             attn_copy.start()
-        if not waited and t >= 3:
+        if t == 1:
             for copy in weights:
                 copy.wait()
-            waited = True
-        if 1 <= t - 2 <= parts:
-            k = t - 3
-            if waited:
-                project(c * parts + k, k == 0)
-        if 1 <= t - 3 <= parts:
-            k = t - 4
+        if 0 <= t - 1 < parts:
+            project(c * parts + t - 1, t == 1)
+        if 0 <= t - 2 < parts:
+            k = t - 2
             g = other * parts + k
             arrived(xs.at[g], gs_s.at[k], gs_r.at[k], sib_id)
             project(g, False)
@@ -367,6 +381,7 @@
 def fused(parts, *args):
     (q_latent, q_rope, cache_latent, cache_rope, cache_len, stream, norm_gain,
      expert_ids, route_weights, w_gate, w_up, w_down) = args
+    q_rope, cache_rope = q_rope.swapaxes(1, 2), cache_rope.swapaxes(1, 2)
     rows, width = stream.shape
     half = width // 2
     chunk = half // parts
@@ -388,8 +403,8 @@
         vm((parts, 4, 4, pair, chunk), bf), vm((parts, 4, 4, pair, chunk), bf),
         vm((parts, 2, 2, pair, chunk), bf), vm((parts, 2, 4, pair, chunk), bf),
         vm((parts, 3, pair, chunk), bf), vm((parts, 2, rows, chunk), fl), vm((parts, rows, chunk), fl),
-        dma((5,)), dma((3 * local,)), dma((2,)),
-        dma((parts + 1, 3)), dma((parts + 1, 3)), dma((parts + 1, 2)), dma((parts + 1, 2)),
+        dma((5,)), dma((3 * local,)), dma((2,)), dma((4,)), dma((4,)),
+        dma((parts + 1, 3)), dma((parts + 1, 3)), dma((parts + 1, 6)), dma((parts + 1, 6)),
         dma((parts + 1, 2)), dma((parts + 1, 2)), dma((parts,)), dma((parts,)),
         dma((parts,)), dma((parts,)), dma((parts, 2)), dma((parts, 2)),
         dma((parts, 2)), dma((parts, 2)), dma((parts, 3)), dma((parts, 3)),

time: 77 us -> 66.4 us (0.86)
  Pallas kernels: 68.9 us -> 61.7 us
  local copies, waits for them, and re-layouts: 7.31 us -> 3.81 us
    pallas_call x1, Pallas kernels: 68.9 us -> 61.7 us  [fused(): pl.pallas_call(functools.partial(fused_kernel, parts), out_shape=(jax.Sha...]
    unnamed x4 -> x2, local copies, waits for them, and re-layouts: 7.31 us -> 3.81 us
where the time goes in v2:
time: 66.4 us; the launch traced here: 66.2 us
  Pallas kernels  61.7 us (93%)
  local copies, waits for them, and re-layouts  3.81 us (6%)
    pallas_call x1, Pallas kernels, fused(): pl.pallas_call(functools.partial(fused_kernel, parts), out_shape=(jax.Sha...  61.7 us
    unnamed x2, local copies, waits for them, and re-layouts  3.81 us

profile of v2, /device:TPU:1, one launch (start us, length us, event | category | flops | bytes accessed | tf_op | source)
XLA Modules:
  0.0 66.2 jit_solution(18151454970193675586)
XLA Ops:
  0.6 61.7 %shard_map.131 = (bf16[8,128,512]{2,1,0:T(8,128)(2,1)}, bf16[8,7168]{1,0:T(8,128)(2,1)}) custom-call(bf16[8,128,512]{2,1,0:T(8,128)(2,1)} %ql_hbm.1, bf16[8,64,128]{2,1,0:T(8,128)(2,1)} %bitcast.3, bf16[8,128,512]{2,1,0:T(8,128)(2,1)} %cl_hbm.1, bf16[8,64,128]{2,1,0:T(8,128)(2,1)} %bitcast.4, s32[8]{0:T(128)} %len_ref.1, bf16[8,7168]{1,0:T(8,128)(2,1)} %stream_ref.1, ...), custom_call_target="tpu_custom_call" | custom-call | tf_op jit(solution)/shard_map/pallas_call | solution.py:413
  62.4 2.3 %copy.16 = bf16[8,128,512]{2,1,0:T(8,128)(2,1)} copy(bf16[8,128,512]{2,1,0:T(8,128)(2,1)} %get-tuple-element.4) | data formatting | bytes 2097152
  64.6 1.6 %copy.17 = bf16[8,7168]{1,0:T(8,128)(2,1)} copy(bf16[8,7168]{1,0:T(8,128)(2,1)} %get-tuple-element.5) | data formatting | bytes 229376
